TPU v7x, 32 devices: a whole 2x2x4 slice. The times are simulated.
32 devices in a mesh: section: 4 (over x, core), expert: 4 (over z), dp: 2 (over y).
Axes of the slice: x: 2, y: 2, z: 4, core: 2. Of those that a mesh axis runs over, the one named last changes fastest.
Arguments:
- tokens: bfloat16 [2, 512, 3072], P(None, ('expert', 'dp')), may hold values from -6 to 6
- routes: int32 [2, 512, 2], P(None, ('expert', 'dp')), may hold values from 0 to 3, all different within a row; in each aligned block of 64 rows (0 to 63, 64 to 127, ..., all dimensions but the last counted through in order) at most 36 rows name the same one
- router: bfloat16 [3072, 4], replicated, may hold values from -0.109375 to 0.109375
- gate_weight: bfloat16 [4, 8192, 3072], P('expert', ('section', 'dp')), may hold values from -0.109375 to 0.109375
- up_weight: bfloat16 [4, 8192, 3072], P('expert', ('section', 'dp')), may hold values from -0.109375 to 0.109375
- down_weight: bfloat16 [4, 8192, 3072], P('expert', ('section', 'dp')), may hold values from -0.0625 to 0.0625
Outputs:
- activations: bfloat16 [2, 512, 3072], P(None, ('expert', 'dp'), 'section')
- gram: bfloat16 [4, 3072, 3072], P('expert', ('section', 'dp'))
Inputs may be any that keep to these rules, and one draw needn't show every extreme that they name: `routes`: in every micro-batch, each aligned block of 64 tokens (the tokens of one device) names no expert more than 36 times, a bound that some block reaches; the two experts of a token differ; every expert is named somewhere.
All inputs are finite; a program needn't handle non-finite values.
Results may differ from a plain program's by a relative error of at most 0.02.
Values may be sent and summed in bfloat16 or wider, within the bound.
A program may use at most 128 MiB of HBM per device.

v0:
```python
import jax
import jax.numpy as jnp
from jax import lax
from jax.sharding import PartitionSpec as P


def route_targets(route_ids, experts, capacity):
    onehot = (route_ids[:, :, None] == jnp.arange(experts, dtype=jnp.int32)[None, None, :]).astype(
        jnp.int32
    )
    flattened = onehot.reshape(-1, experts)
    before = jnp.cumsum(flattened, axis=0) - flattened
    slot_rank = jnp.sum(before * flattened, axis=1).reshape(route_ids.shape)
    return route_ids * capacity + slot_rank


def on_device(tokens, routes, router, gate_weight, up_weight, down_weight):
    micro_count = tokens.shape[0]
    rows_dev = tokens.shape[1]
    model_width = tokens.shape[2]
    experts = router.shape[1]
    capacity = 9 * rows_dev // (4 * experts)
    section_count = lax.axis_size("section")
    replicas = lax.axis_size("dp")
    section_index = lax.axis_index("section")
    col_width = model_width // section_count
    gate_rows = gate_weight[0]
    up_rows = up_weight[0]
    down_rows = down_weight[0]
    logits = jnp.einsum("mtd,de->mte", tokens, router, preferred_element_type=jnp.float32)
    chosen = jnp.take_along_axis(logits, routes, axis=-1)
    logit_gap = chosen[..., 0] - chosen[..., 1]
    first_gate = jax.nn.sigmoid(logit_gap)
    second_gate = jax.nn.sigmoid(-logit_gap)
    target = jax.vmap(lambda one_block: route_targets(one_block, experts, capacity))(routes)
    slot_ids = jnp.arange(experts * capacity, dtype=jnp.int32)
    placing = jnp.sum(
        (slot_ids[None, :, None, None] == target[:, None, :, :]).astype(jnp.float32), axis=3
    ).astype(jnp.bfloat16)
    outgoing = jnp.einsum(
        "mst,mtd->msd", placing, tokens, preferred_element_type=jnp.float32
    ).astype(jnp.bfloat16)
    outgoing = outgoing.reshape(micro_count, experts, capacity, model_width)
    arrived = lax.all_to_all(outgoing, "expert", split_axis=1, concat_axis=1, tiled=True)
    rows_all = arrived.reshape(-1, model_width)
    gate_piece = lax.all_gather(gate_rows, "dp", axis=0, tiled=True)
    up_piece = lax.all_gather(up_rows, "dp", axis=0, tiled=True)
    down_piece = lax.all_gather(down_rows, "dp", axis=0, tiled=True)
    gate_part = lax.dot_general(
        rows_all, gate_piece, (((1,), (1,)), ((), ())), preferred_element_type=jnp.float32
    )
    up_part = lax.dot_general(
        rows_all, up_piece, (((1,), (1,)), ((), ())), preferred_element_type=jnp.float32
    )
    inner_units = (jax.nn.silu(gate_part) * up_part).astype(jnp.bfloat16)
    partial_out = jnp.dot(inner_units, down_piece, preferred_element_type=jnp.float32)
    summed_out = lax.psum_scatter(
        partial_out.astype(jnp.bfloat16), "section", scatter_dimension=1, tiled=True
    )
    expert_out = summed_out.reshape(micro_count, experts, capacity, col_width)
    returned = lax.all_to_all(expert_out, "expert", split_axis=1, concat_axis=1, tiled=True)
    flat_back = returned.reshape(micro_count, experts * capacity, col_width)
    first_rows = jnp.take_along_axis(flat_back, target[:, :, 0][:, :, None], axis=1).astype(
        jnp.float32
    )
    second_rows = jnp.take_along_axis(flat_back, target[:, :, 1][:, :, None], axis=1).astype(
        jnp.float32
    )
    own_cols = lax.dynamic_slice_in_dim(tokens, section_index * col_width, col_width, 2).astype(
        jnp.float32
    )
    layer_out = (
        own_cols + first_gate[..., None] * first_rows + second_gate[..., None] * second_rows
    ).astype(jnp.bfloat16)
    all_tokens = rows_dev * lax.axis_size("expert") * replicas
    gram_scale = experts / (2.0 * micro_count * all_tokens)
    block_rows = col_width // replicas
    left_cols = lax.dynamic_slice_in_dim(
        rows_all, section_index * col_width, block_rows * lax.axis_size("dp"), 1
    )
    product = (
        lax.dot_general(
            left_cols, rows_all, (((0,), (0,)), ((), ())), preferred_element_type=jnp.float32
        )
        * gram_scale
    )
    rounded = lax.optimization_barrier(product.astype(jnp.bfloat16))
    gram_block = lax.psum_scatter(
        rounded.astype(jnp.float32).astype(jnp.bfloat16), "dp", scatter_dimension=0, tiled=True
    )
    return (layer_out, gram_block[None])


def solution(mesh):
    return jax.shard_map(
        on_device,
        mesh=mesh,
        in_specs=(
            P(None, ("expert", "dp"), None),
            P(None, ("expert", "dp"), None),
            P(),
            P("expert", ("section", "dp"), None),
            P("expert", ("section", "dp"), None),
            P("expert", ("section", "dp"), None),
        ),
        out_specs=(P(None, ("expert", "dp"), "section"), P("expert", ("section", "dp"), None)),
        check_vma=False,
    )
```

profile of v0, /device:TPU:0, one launch (start us, length us, event | category | flops | bytes accessed | tf_op | source)
XLA Modules:
  0.0 586.5 jit_solution(679741173083976250)
XLA Ops:
  7.2 0.7 all-gather.7.cloned.1.call-update
  8.0 0.7 all-gather.11.cloned.1.call-update
  8.7 0.7 all-gather.9.cloned.1.call-update
  10.6 0.7 convolution_convert_fusion
  11.2 1.8 copy.70
  13.1 47.3 %all_to_all.10 = bf16[2,4,36,3072]{3,0,2,1:T(2,128)(2,1)S(1)} all-to-all(bf16[2,4,36,3072]{3,0,2,1:T(2,128)(2,1)S(1)} %bitcast.45), channel_id=1, replica_groups=mesh['section'=4,'expert'=4,'dp'=2] {'expert'}, dimensions={1} | all-to-all | bytes 3538944 | tf_op jit(solution)/shard_map/all_to_all | solution.py:44
  60.4 0.4 copy.71
  60.8 1.4 reshape.37
  62.2 102.7 %all-gather.7.cloned.1.call-done = bf16[1,2048,3072]{2,1,0:T(8,128)(2,1)} async-done(((bf16[1,1024,3072]{2,1,0:T(8,128)(2,1)}), bf16[1,2048,3072]{2,1,0:T(8,128)(2,1)}) %all-gather.7.cloned.1.call-update) | async-done | bytes 12582928 | tf_op jit(solution)/shard_map/all_gather | solution.py:46
  164.8 10.4 %fusion.4 = f32[288,2048]{1,0:T(8,128)} fusion(bf16[288,3072]{1,0:T(8,128)(2,1)} %reshape.37, bf16[1,2048,3072]{2,1,0:T(8,128)(2,1)} %all-gather.7.cloned.1.call-done), kind=kOutput, calls=%fused_computation.7 | convolution fusion | flops 3623878656 | bytes 16711680 | tf_op jit(solution)/shard_map/dot_general | solution.py:49
  175.3 143.7 %all-gather.11.cloned.1.call-done = bf16[1,2048,3072]{2,1,0:T(8,128)(2,1)} async-done(((bf16[1,1024,3072]{2,1,0:T(8,128)(2,1)}), bf16[1,2048,3072]{2,1,0:T(8,128)(2,1)}) %all-gather.11.cloned.1.call-update) | async-done | bytes 12582928 | tf_op jit(solution)/shard_map/all_gather | solution.py:48
  318.9 154.1 %all-gather.9.cloned.1.call-done = bf16[1,2048,3072]{2,1,0:T(8,128)(2,1)} async-done(((bf16[1,1024,3072]{2,1,0:T(8,128)(2,1)}), bf16[1,2048,3072]{2,1,0:T(8,128)(2,1)}) %all-gather.9.cloned.1.call-update) | async-done | bytes 12582928 | tf_op jit(solution)/shard_map/all_gather | solution.py:47
  473.1 14.5 %fusion.6 = bf16[288,3072]{1,0:T(8,128)(2,1)} fusion(bf16[1,2048,3072]{2,1,0:T(8,128)(2,1)} %all-gather.11.cloned.1.call-done, bf16[288,3072]{1,0:T(8,128)(2,1)S(1)} %copy-done.2, bf16[1,2048,3072]{2,1,0:T(8,128)(2,1)} %all-gather.9.cloned.1.call-done, f32[288,2048]{1,0:T(8,128)} %fusion.4), kind=kOutput, calls=%fused_computation.11 | convolution fusion | flops 7252180992 | bytes 31064064 | tf_op jit(solution)/shard_map/dot_general | solution.py:56
  487.8 4.4 multiply_convert_fusion
  493.1 2.8 gather_fusion
  496.2 20.9 %reduce-scatter.3.cloned.1.call-done = bf16[288,768]{1,0:T(8,128)(2,1)} async-done(((bf16[288,3072]{1,0:T(8,128)(2,1)}), bf16[288,768]{1,0:T(8,128)(2,1)}) %reduce-scatter.3.cloned.1.call-update) | async-done | bytes 442384 | tf_op jit(solution)/shard_map/reduce_scatter | solution.py:57
  517.1 1.1 reshape.38
  518.2 1.2 copy.72
  519.5 4.6 all-to-all-start.1
  524.1 12.7 %all-to-all-done.1 = bf16[2,4,36,768]{3,0,2,1:T(2,128)(2,1)S(1)} async-done(((bf16[2,4,36,768]{3,0,2,1:T(2,128)(2,1)}), bf16[2,4,36,768]{3,0,2,1:T(2,128)(2,1)S(1)}, u32[]{:S(2)}, u32[]{:S(2)}) %all-to-all-start.1) | async-done | bytes 442400 | tf_op jit(solution)/shard_map/all_to_all | solution.py:61
  536.9 1.5 gather_fusion.1
  538.4 1.5 gather_fusion.2
  539.8 0.9 add_convert_fusion
  540.7 39.2 %reduce-scatter.5.cloned.1.call-done = bf16[384,3072]{1,0:T(8,128)(2,1)} async-done(((bf16[768,3072]{1,0:T(8,128)(2,1)}), bf16[384,3072]{1,0:T(8,128)(2,1)}) %reduce-scatter.5.cloned.1.call-update) | async-done | bytes 2359312 | tf_op jit(solution)/shard_map/reduce_scatter | solution.py:88
  (38 shorter events, 2.6 us)
Async XLA Ops:
  7.2 485.6 %copy-start = (bf16[3072,4]{0,1:T(4,128)(2,1)S(1)}, bf16[3072,4]{0,1:T(4,128)(2,1)}, u32[]{:S(2)}) copy-start(bf16[3072,4]{0,1:T(4,128)(2,1)} %param.10) | copy-start | bytes 73732
  7.2 157.6 %all-gather.7.cloned.1.call-start = ((), (), s32[]{:S(2)}) async-start(), calls=%async_computation.6 | async-start | bytes 18874368 | tf_op jit(solution)/shard_map/all_gather | solution.py:46
  7.9 311.0 %all-gather.11.cloned.1.call-start = ((), (), s32[]{:S(2)}) async-start(), calls=%async_computation.8 | async-start | bytes 18874368 | tf_op jit(solution)/shard_map/all_gather | solution.py:48
  8.7 0.8 copy-start.3
  8.7 1.9 copy-start.1
  8.7 464.4 %all-gather.9.cloned.1.call-start = ((), (), s32[]{:S(2)}) async-start(), calls=%async_computation.7 | async-start | bytes 18874368 | tf_op jit(solution)/shard_map/all_gather | solution.py:47
  9.4 507.7 %reduce-scatter.3.cloned.1.call-start = ((), (), s32[]{:S(2)}) async-start(), calls=%async_computation.4 | async-start | bytes 2211840 | tf_op jit(solution)/shard_map/reduce_scatter | solution.py:57
  62.2 410.9 %copy-start.2 = (bf16[288,3072]{1,0:T(8,128)(2,1)S(1)}, bf16[288,3072]{1,0:T(8,128)(2,1)}, u32[]{:S(2)}) copy-start(bf16[288,3072]{1,0:T(8,128)(2,1)} %reshape.37) | copy-start | bytes 5308420
  487.6 92.4 %reduce-scatter.5.cloned.1.call-start = ((), (), s32[]{:S(2)}) async-start(), calls=%async_computation.5 | async-start | bytes 7077888 | tf_op jit(solution)/shard_map/reduce_scatter | solution.py:88
  519.5 17.3 %all-to-all-start.1 = ((bf16[2,4,36,768]{3,0,2,1:T(2,128)(2,1)}), bf16[2,4,36,768]{3,0,2,1:T(2,128)(2,1)S(1)}, u32[]{:S(2)}, u32[]{:S(2)}) async-start(bf16[2,4,36,768]{3,0,2,1:T(2,128)(2,1)} %copy.72), calls=%async_computation.2 | async-start | bytes 884736 | tf_op jit(solution)/shard_map/all_to_all | solution.py:61
Sparse Core Ops, SparseCore 0:
  9.6 155.2 all-gather.6
  166.4 152.5 all-gather.10
  320.5 152.5 all-gather.8
  487.7 29.3 reduce-scatter.2
  519.9 59.9 reduce-scatter.4
where the time goes:
time: 587 us
  waiting for transfers between devices  475 us (81%)
  blocking collectives  47.3 us (8%)
  matrix products  30.4 us (5%)
  between operations  14 us (2%)
  local copies, waits for them, and re-layouts  12.9 us (2%)
    all_gather x1, waiting for transfers between devices, on_device(): up_piece = lax.all_gather(up_rows, 'dp', axis=0, tiled=True)  154 us
    all_gather x1, waiting for transfers between devices, on_device(): down_piece = lax.all_gather(down_rows, 'dp', axis=0, tiled=True)  144 us
    all_gather x1, waiting for transfers between devices, on_device(): gate_piece = lax.all_gather(gate_rows, 'dp', axis=0, tiled=True)  103 us
    all_to_all x1, blocking collectives, on_device(): lax.all_to_all(outgoing, 'expert', split_axis=1, concat_axis=1, tiled=True)  47.3 us
    reduce_scatter x1, waiting for transfers between devices, on_device(): lax.psum_scatter(rounded.astype(jnp.float32).astype(jnp.bfloat16), 'dp',...  39.2 us
    reduce_scatter x1, waiting for transfers between devices, on_device(): lax.psum_scatter(partial_out.astype(jnp.bfloat16), 'section', scatter_dim...  20.9 us
    dot_general x1, matrix products, on_device(): jnp.dot(inner_units, down_piece, preferred_element_type=jnp.float32)  14.5 us
    all_to_all x1, waiting for transfers between devices, on_device(): lax.all_to_all(expert_out, 'expert', split_axis=1, concat_axis=1, tiled=T...  12.7 us
  transfers between devices with their start and end apart: 6, of which 6 were waited for; matrix products, arithmetic and copies ran while one was open for 5% of the time, Pallas kernels for 0%

commit v1 on v0

--- a/solution.py
+++ b/solution.py
@@ -9,7 +9,11 @@
         jnp.int32
     )
     flattened = onehot.reshape(-1, experts)
-    before = jnp.cumsum(flattened, axis=0) - flattened
+    pairs = jnp.arange(flattened.shape[0], dtype=jnp.int32)
+    earlier = (pairs[None, :] < pairs[:, None]).astype(jnp.bfloat16)
+    before = jnp.dot(
+        earlier, flattened.astype(jnp.bfloat16), preferred_element_type=jnp.float32
+    ).astype(jnp.int32)
     slot_rank = jnp.sum(before * flattened, axis=1).reshape(route_ids.shape)
     return route_ids * capacity + slot_rank
 
@@ -43,20 +47,19 @@
     outgoing = outgoing.reshape(micro_count, experts, capacity, model_width)
     arrived = lax.all_to_all(outgoing, "expert", split_axis=1, concat_axis=1, tiled=True)
     rows_all = arrived.reshape(-1, model_width)
-    gate_piece = lax.all_gather(gate_rows, "dp", axis=0, tiled=True)
-    up_piece = lax.all_gather(up_rows, "dp", axis=0, tiled=True)
-    down_piece = lax.all_gather(down_rows, "dp", axis=0, tiled=True)
+    rows_both = lax.all_gather(rows_all, "dp", axis=0, tiled=True)
     gate_part = lax.dot_general(
-        rows_all, gate_piece, (((1,), (1,)), ((), ())), preferred_element_type=jnp.float32
+        rows_both, gate_rows, (((1,), (1,)), ((), ())), preferred_element_type=jnp.float32
     )
     up_part = lax.dot_general(
-        rows_all, up_piece, (((1,), (1,)), ((), ())), preferred_element_type=jnp.float32
+        rows_both, up_rows, (((1,), (1,)), ((), ())), preferred_element_type=jnp.float32
     )
     inner_units = (jax.nn.silu(gate_part) * up_part).astype(jnp.bfloat16)
-    partial_out = jnp.dot(inner_units, down_piece, preferred_element_type=jnp.float32)
+    partial_out = jnp.dot(inner_units, down_rows, preferred_element_type=jnp.float32)
     summed_out = lax.psum_scatter(
         partial_out.astype(jnp.bfloat16), "section", scatter_dimension=1, tiled=True
     )
+    summed_out = lax.psum_scatter(summed_out, "dp", scatter_dimension=0, tiled=True)
     expert_out = summed_out.reshape(micro_count, experts, capacity, col_width)
     returned = lax.all_to_all(expert_out, "expert", split_axis=1, concat_axis=1, tiled=True)
     flat_back = returned.reshape(micro_count, experts * capacity, col_width)
@@ -75,19 +78,16 @@
     all_tokens = rows_dev * lax.axis_size("expert") * replicas
     gram_scale = experts / (2.0 * micro_count * all_tokens)
     block_rows = col_width // replicas
+    per_replica = rows_both.reshape(replicas, -1, model_width)
     left_cols = lax.dynamic_slice_in_dim(
-        rows_all, section_index * col_width, block_rows * lax.axis_size("dp"), 1
+        per_replica, (section_index * replicas + lax.axis_index("dp")) * block_rows, block_rows, 2
     )
     product = (
-        lax.dot_general(
-            left_cols, rows_all, (((0,), (0,)), ((), ())), preferred_element_type=jnp.float32
-        )
+        jnp.einsum("nrd,nrf->ndf", left_cols, per_replica, preferred_element_type=jnp.float32)
         * gram_scale
     )
     rounded = lax.optimization_barrier(product.astype(jnp.bfloat16))
-    gram_block = lax.psum_scatter(
-        rounded.astype(jnp.float32).astype(jnp.bfloat16), "dp", scatter_dimension=0, tiled=True
-    )
+    gram_block = jnp.sum(rounded.astype(jnp.float32), axis=0).astype(jnp.bfloat16)
     return (layer_out, gram_block[None])
 
 

time: 587 us -> 225 us (0.38)
  waiting for transfers between devices: 475 us -> 106 us
    all_gather x3 -> x1, waiting for transfers between devices: 400 us -> 48.7 us  [on_device(): rows_both = lax.all_gather(rows_all, 'dp', axis=0, tiled=True)]
    reduce_scatter x1, waiting for transfers between devices: 39.2 us -> 16.9 us  [on_device(): lax.psum_scatter(summed_out, 'dp', scatter_dimension=0, tiled=True)]
    reduce_scatter x1, waiting for transfers between devices: 20.9 us -> 40.4 us  [on_device(): lax.psum_scatter(partial_out.astype(jnp.bfloat16), 'section', scatter_dim...]
    all_to_all x1, waiting for transfers between devices: 12.7 us -> 0.33 us  [on_device(): lax.all_to_all(expert_out, 'expert', split_axis=1, concat_axis=1, tiled=T...]
  transfers between devices with their start and end apart: 6 -> 4, of which waited for: 6 -> 4; matrix products, arithmetic and copies ran while one was open for 5% -> 7% of each run, Pallas kernels for 0% -> 0%
where the time goes in v1:
time: 225 us
  waiting for transfers between devices  106 us (47%)
  blocking collectives  47.3 us (21%)
  matrix products  31.4 us (14%)
  between operations  13.9 us (6%)
  local copies, waits for them, and re-layouts  13.6 us (6%)
  other arithmetic  7.26 us (3%)
  starting transfers between devices  4.9 us (2%)
    all_gather x1, waiting for transfers between devices, on_device(): rows_both = lax.all_gather(rows_all, 'dp', axis=0, tiled=True)  48.7 us
    all_to_all x1, blocking collectives, on_device(): lax.all_to_all(outgoing, 'expert', split_axis=1, concat_axis=1, tiled=True)  47.3 us
    reduce_scatter x1, waiting for transfers between devices, on_device(): lax.psum_scatter(partial_out.astype(jnp.bfloat16), 'section', scatter_dim...  40.4 us
    reduce_scatter x1, waiting for transfers between devices, on_device(): lax.psum_scatter(summed_out, 'dp', scatter_dimension=0, tiled=True)  16.9 us
    dot_general x1, matrix products, on_device(): jnp.dot(inner_units, down_rows, preferred_element_type=jnp.float32)  15.1 us
    dot_general x1, matrix products, on_device(): lax.dot_general(rows_both, up_rows, (((1,), (1,)), ((), ())), preferred_e...  7.04 us
    dot_general x1, matrix products, on_device(): jnp.einsum('nrd,nrf->ndf', left_cols, per_replica, preferred_element_type...  6.93 us
    reduce_sum x1, other arithmetic, on_device(): jnp.sum(rounded.astype(jnp.float32), axis=0).astype(jnp.bfloat16)  5.46 us
  transfers between devices with their start and end apart: 4, of which 4 were waited for; matrix products, arithmetic and copies ran while one was open for 7% of the time, Pallas kernels for 0%

profile of v1, /device:TPU:0, one launch (start us, length us, event | category | flops | bytes accessed | tf_op | source)
XLA Modules:
  0.0 224.7 jit_solution(2923301301395729862)
XLA Ops:
  7.2 0.8 copy.68
  8.6 0.7 multiply_add_fusion
  9.4 1.8 convolution_convert_fusion
  11.2 1.8 copy.70
  13.0 47.3 %all_to_all.10 = bf16[2,4,36,3072]{3,0,2,1:T(2,128)(2,1)S(1)} all-to-all(bf16[2,4,36,3072]{3,0,2,1:T(2,128)(2,1)S(1)} %bitcast.53), channel_id=1, replica_groups=mesh['section'=4,'expert'=4,'dp'=2] {'expert'}, dimensions={1} | all-to-all | bytes 3538944 | tf_op jit(solution)/shard_map/all_to_all | solution.py:48
  60.3 0.4 copy.71
  60.7 1.4 reshape.40
  62.2 48.7 %all-gather.2.cloned.1.call-done = bf16[576,3072]{1,0:T(8,128)(2,1)} async-done(((bf16[288,3072]{1,0:T(8,128)(2,1)}), bf16[576,3072]{1,0:T(8,128)(2,1)}) %all-gather.2.cloned.1.call-update) | async-done | bytes 3538960 | tf_op jit(solution)/shard_map/all_gather | solution.py:50
  110.8 7.0 %fusion.2 = f32[576,1024]{1,0:T(8,128)S(1)} fusion(bf16[576,3072]{1,0:T(8,128)(2,1)} %all-gather.2.cloned.1.call-done, bf16[1,1024,3072]{2,1,0:T(8,128)(2,1)} %param.12), kind=kOutput, calls=%fused_computation.6 | convolution fusion | flops 3623878656 | bytes 12189696 | tf_op jit(solution)/shard_map/dot_general | solution.py:54
  117.9 15.1 %fusion.6 = bf16[576,3072]{1,0:T(8,128)(2,1)} fusion(bf16[1,1024,3072]{2,1,0:T(8,128)(2,1)} %param.13, f32[576,1024]{1,0:T(8,128)S(1)} %fusion.2, bf16[576,3072]{1,0:T(8,128)(2,1)} %all-gather.2.cloned.1.call-done, bf16[1,1024,3072]{2,1,0:T(8,128)(2,1)} %param.11), kind=kOutput, calls=%fused_computation.10 | convolution fusion | flops 7253065728 | bytes 22020096 | tf_op jit(solution)/shard_map/dot_general | solution.py:58
  133.1 0.2 reduce-scatter.5.cloned.1.call-start
  133.3 40.4 %reduce-scatter.3.cloned.1.call-done = bf16[576,768]{1,0:T(8,128)(2,1)} async-done(((bf16[576,3072]{1,0:T(8,128)(2,1)}), bf16[576,768]{1,0:T(8,128)(2,1)}) %reduce-scatter.3.cloned.1.call-update) | async-done | bytes 884752 | tf_op jit(solution)/shard_map/reduce_scatter | solution.py:59
  174.2 0.4 fusion.16
  174.6 2.8 %gather_fusion = f32[256]{0:T(256)S(1)} fusion(f32[2,64,4]{1,2,0:T(4,128)S(1)} %fusion.16, s32[256]{0:T(256)S(1)} %reshape.56), kind=kCustom, calls=%fused_computation.2 | custom fusion | bytes 5120 | tf_op jit(solution)/shard_map/jit(take_along_axis)/gather | solution.py:35
  177.7 16.9 %reduce-scatter.5.cloned.1.call-done = bf16[288,768]{1,0:T(8,128)(2,1)} async-done(((bf16[576,768]{1,0:T(8,128)(2,1)}), bf16[288,768]{1,0:T(8,128)(2,1)}) %reduce-scatter.5.cloned.1.call-update) | async-done | bytes 442384 | tf_op jit(solution)/shard_map/reduce_scatter | solution.py:62
  194.6 1.1 reshape.41
  195.7 1.3 copy.72
  196.9 4.6 %all-to-all-start.1 = ((bf16[2,4,36,768]{3,0,2,1:T(2,128)(2,1)}), bf16[2,4,36,768]{3,0,2,1:T(2,128)(2,1)S(1)}, u32[]{:S(2)}, u32[]{:S(2)}) async-start(bf16[2,4,36,768]{3,0,2,1:T(2,128)(2,1)} %copy.72), calls=%async_computation.3 | async-start | bytes 884736 | tf_op jit(solution)/shard_map/all_to_all | solution.py:64
  201.6 6.9 %multiply_convert_fusion = bf16[2,384,3072]{2,1,0:T(8,128)(2,1)} fusion(bf16[2,288,3072]{2,1,0:T(8,128)(2,1)} %bitcast.60, s32[]{:T(128)S(6)} %select_n.23), kind=kOutput, calls=%fused_computation.3 | convolution fusion | flops 1363673088 | bytes 8699908 | tf_op jit(solution)/shard_map/nrd,nrf->ndf/dot_general | solution.py:86
  208.5 5.5 %reduce_sum.32 = bf16[384,3072]{1,0:T(8,128)(2,1)} reduce(bf16[2,384,3072]{2,1,0:T(8,128)(2,1)} %multiply_convert_fusion, bf16[]{:T(256)} %constant.55.clone.1), dimensions={0}, to_apply=%region_4.6 | reduce | flops 1179648 | bytes 7077890 | tf_op jit(solution)/shard_map/reduce_sum | solution.py:90
  213.9 0.3 all-to-all-done.1
  214.3 1.5 gather_fusion.1
  215.8 1.5 gather_fusion.2
  217.3 0.9 add_convert_fusion
  (31 shorter events, 1.5 us)
Async XLA Ops:
  7.2 167.0 %copy-start = (bf16[3072,4]{0,1:T(4,128)(2,1)S(1)}, bf16[3072,4]{0,1:T(4,128)(2,1)}, u32[]{:S(2)}) copy-start(bf16[3072,4]{0,1:T(4,128)(2,1)} %param.10) | copy-start | bytes 73732
  7.2 103.7 %all-gather.2.cloned.1.call-start = ((), (), s32[]{:S(2)}) async-start(), calls=%async_computation.4 | async-start | bytes 5308416 | tf_op jit(solution)/shard_map/all_gather | solution.py:50
  62.1 111.5 %reduce-scatter.3.cloned.1.call-start = ((), (), s32[]{:S(2)}) async-start(), calls=%async_computation.5 | async-start | bytes 4423680 | tf_op jit(solution)/shard_map/reduce_scatter | solution.py:59
  133.0 40.9 %copy-start.2 = (s32[2,64,2]{1,2,0:T(2,128)S(1)}, s32[2,64,2]{1,2,0:T(2,128)}, u32[]{:S(2)}) copy-start(s32[2,64,2]{1,2,0:T(2,128)} %param.9) | copy-start | bytes 3076
  133.0 41.1 %copy-start.1 = (bf16[2,64,3072]{2,1,0:T(8,128)(2,1)S(1)}, bf16[2,64,3072]{2,1,0:T(8,128)(2,1)}, u32[]{:S(2)}) copy-start(bf16[2,64,3072]{2,1,0:T(8,128)(2,1)} %param.8) | copy-start | bytes 2359300
  133.1 61.5 %reduce-scatter.5.cloned.1.call-start = ((), (), s32[]{:S(2)}) async-start(), calls=%async_computation.6 | async-start | bytes 1327104 | tf_op jit(solution)/shard_map/reduce_scatter | solution.py:62
  196.9 17.3 %all-to-all-start.1 = ((bf16[2,4,36,768]{3,0,2,1:T(2,128)(2,1)}), bf16[2,4,36,768]{3,0,2,1:T(2,128)(2,1)S(1)}, u32[]{:S(2)}, u32[]{:S(2)}) async-start(bf16[2,4,36,768]{3,0,2,1:T(2,128)(2,1)} %copy.72), calls=%async_computation.3 | async-start | bytes 884736 | tf_op jit(solution)/shard_map/all_to_all | solution.py:64
Sparse Core Ops, SparseCore 0:
  62.3 48.5 all-gather.1
  133.2 40.4 reduce-scatter.2
  176.0 18.4 reduce-scatter.4

commit v2 on v1

--- a/solution.py
+++ b/solution.py
@@ -1,6 +1,9 @@
+import functools
 import jax
 import jax.numpy as jnp
 from jax import lax
+from jax.experimental import pallas as pl
+from jax.experimental.pallas import tpu as pltpu
 from jax.sharding import PartitionSpec as P
 
 
@@ -91,9 +94,296 @@
     return (layer_out, gram_block[None])
 
 
+BF16, F32 = jnp.bfloat16, jnp.float32
+
+
+def expert_kernel(
+    experts, rows, scale, ob, gate_hbm, up_hbm, down_hbm, ret, gram,
+    xin, gate_v, up_v, down_v, inner, part, from_core, to_x, from_x, to_y, from_y, final, left_t,
+    w_sem, l_sem, z_s, z_r, y_s, y_r, x_s, x_r, c_s, c_r, d_s, d_r, rc_s, rc_r, rx_s, rx_r, ry_s, ry_r, rz_s, rz_r,
+):
+    width = ob.shape[2]
+    half, third = width // 2, width // 6
+    part_cols = width // 4
+    s, e, d = lax.axis_index("section"), lax.axis_index("expert"), lax.axis_index("dp")
+    x, c = s // 2, s % 2
+    core_nb = {"section": x * 2 + 1 - c}
+    x_nb = {"section": (1 - x) * 2 + c}
+    y_nb = {"dp": 1 - d}
+    z_nb = [{"expert": (e + k) % experts} for k in range(experts)]
+    sent = []
+
+    def put(src, dst, send, recv, to):
+        copy = pltpu.make_async_remote_copy(
+            src_ref=src, dst_ref=dst, send_sem=send, recv_sem=recv,
+            device_id=to, device_id_type=pl.DeviceIdType.MESH,
+        )
+        copy.start()
+        sent.append(copy)
+
+    def got(dst, send, recv, to):
+        pltpu.make_async_remote_copy(
+            src_ref=dst, dst_ref=dst, send_sem=send, recv_sem=recv,
+            device_id=to, device_id_type=pl.DeviceIdType.MESH,
+        ).wait_recv()
+
+    weights = [
+        pltpu.make_async_copy(gate_hbm, gate_v, w_sem.at[0]),
+        pltpu.make_async_copy(up_hbm, up_v, w_sem.at[1]),
+        pltpu.make_async_copy(down_hbm, down_v, w_sem.at[2]),
+    ]
+    for copy in weights:
+        copy.start()
+    row_of = lambda src: pl.ds(pl.multiple_of(src * rows, 16), rows)
+    own_copy = pltpu.make_async_copy(ob.at[e], xin.at[d, row_of(e)], l_sem)
+    own_copy.start()
+
+    barrier = pltpu.get_barrier_semaphore()
+    partners = [core_nb, x_nb, y_nb] + z_nb[1:]
+    for to in partners:
+        pl.semaphore_signal(barrier, inc=1, device_id=to, device_id_type=pl.DeviceIdType.MESH)
+    pl.semaphore_wait(barrier, len(partners))
+
+    fetched = pl.ds(pl.multiple_of(c * half + x * third, 128), 2 * third)
+    mine_x = pl.ds(pl.multiple_of(c * half + x * 2 * third, 128), third)
+    theirs_x = pl.ds(pl.multiple_of(c * half + (1 - x) * 2 * third, 128), third)
+    core_fetched = pl.ds(pl.multiple_of((1 - c) * half + x * third, 128), 2 * third)
+    core_x = pl.ds(pl.multiple_of((1 - c) * half + (1 - x) * 2 * third, 128), third)
+    came = [(e + experts - k) % experts for k in range(experts)]
+
+    def at(own, k, cols):
+        return xin.at[d if own else 1 - d, row_of(came[k]), cols]
+
+    for k in range(1, experts):
+        put(
+            ob.at[(e + k) % experts, :, fetched], xin.at[d, row_of(e), fetched],
+            z_s.at[k], z_r.at[k], z_nb[k],
+        )
+    put(ob.at[e, :, fetched], xin.at[d, row_of(e), fetched], y_s.at[0], y_r.at[0], y_nb)
+    for k in range(1, experts):
+        got(at(True, k, fetched), z_s.at[k], z_r.at[k], z_nb[k])
+        put(at(True, k, fetched), at(True, k, fetched), y_s.at[k], y_r.at[k], y_nb)
+        put(at(True, k, mine_x), at(True, k, mine_x), x_s.at[0, k], x_r.at[0, k], x_nb)
+        put(at(True, k, fetched), at(True, k, fetched), c_s.at[0, k], c_r.at[0, k], core_nb)
+    for k in range(1, experts):
+        got(at(True, k, theirs_x), x_s.at[0, k], x_r.at[0, k], x_nb)
+        put(at(True, k, theirs_x), at(True, k, theirs_x), d_s.at[0, k], d_r.at[0, k], core_nb)
+
+    def y_arrival(k):
+        got(at(False, k, fetched), y_s.at[k], y_r.at[k], y_nb)
+        put(at(False, k, mine_x), at(False, k, mine_x), x_s.at[1, k], x_r.at[1, k], x_nb)
+        put(at(False, k, fetched), at(False, k, fetched), c_s.at[1, k], c_r.at[1, k], core_nb)
+
+    def all_here(p):
+        for k in range(1 - p, experts):
+            own = p == 0
+            got(at(own, k, core_fetched), c_s.at[p, k], c_r.at[p, k], core_nb)
+            got(at(own, k, core_x), d_s.at[p, k], d_r.at[p, k], core_nb)
+
+    tile = 256
+    steps = gate_v.shape[0] // tile
+
+    def hidden(which, h):
+        place = pl.ds(pl.multiple_of(h * tile, tile), tile)
+        nt = (((1,), (1,)), ((), ()))
+        g = lax.dot_general(xin[which], gate_v[place, :], nt, preferred_element_type=F32)
+        u = lax.dot_general(xin[which], up_v[place, :], nt, preferred_element_type=F32)
+        inner[:, place] = (g / (1.0 + jnp.exp(-g)) * u).astype(BF16)
+
+    def outputs(p, section):
+        def step(j, carry):
+            place = pl.ds(pl.multiple_of(j * tile, tile), tile)
+            cols = pl.ds(pl.multiple_of(section * part_cols + j * tile, tile), tile)
+            part[p, section, :, place] = jnp.dot(
+                inner[...], down_v[:, cols], preferred_element_type=F32
+            ).astype(BF16)
+            return carry
+
+        lax.fori_loop(0, part_cols // tile, step, 0)
+
+    def project(p):
+        for far in (0, 1):
+            block = ((1 - x) if far == 0 else x)
+            outputs(p, 2 * block + 1 - c)
+            put(
+                part.at[p, 2 * block + 1 - c], from_core.at[p, far],
+                rc_s.at[p, far], rc_r.at[p, far], core_nb,
+            )
+        outputs(p, 2 * (1 - x) + c)
+        outputs(p, 2 * x + c)
+
+    chunks = list(range(1, experts)) + [0]
+
+    def send_x(p):
+        got(from_core.at[p, 0], rc_s.at[p, 0], rc_r.at[p, 0], core_nb)
+        for k in chunks:
+            r = row_of((e + k) % experts)
+            to_x[p, r, :] = (
+                part[p, 2 * (1 - x) + c, r, :].astype(F32) + from_core[p, 0, r, :].astype(F32)
+            ).astype(BF16)
+            put(to_x.at[p, r], from_x.at[p, r], rx_s.at[p, k], rx_r.at[p, k], x_nb)
+
+    own_copy.wait()
+    for copy in weights:
+        copy.wait()
+    all_here(0)
+    for k in range(experts):
+        if k < steps:
+            hidden(d, k)
+        y_arrival(k)
+    for h in range(experts, steps):
+        hidden(d, h)
+    project(0)
+    for k in range(experts):
+        got(at(False, k, theirs_x), x_s.at[1, k], x_r.at[1, k], x_nb)
+        put(at(False, k, theirs_x), at(False, k, theirs_x), d_s.at[1, k], d_r.at[1, k], core_nb)
+    send_x(0)
+    all_here(1)
+
+    def hidden_step(h, carry):
+        hidden(1 - d, h)
+        return carry
+
+    lax.fori_loop(0, steps, hidden_step, 0)
+    project(1)
+    send_x(1)
+
+    block_rows = gram.shape[0]
+    left = pl.ds(pl.multiple_of((s * 2 + d) * block_rows, 128), block_rows)
+    for r in (0, 1):
+        left_t[r] = xin[r, :, left].astype(F32).T.astype(BF16)
+
+    def gram_step(j, carry):
+        place = pl.ds(pl.multiple_of(j * tile, tile), tile)
+        total = jnp.zeros((block_rows, tile), F32)
+        for r in (0, 1):
+            one = jnp.dot(left_t[r], xin[r, :, place], preferred_element_type=F32) * scale
+            total = total + one.astype(BF16).astype(F32)
+        gram[:, place] = total.astype(BF16)
+        return carry
+
+    lax.fori_loop(0, width // tile, gram_step, 0)
+
+    got(from_core.at[1, 1], rc_s.at[1, 1], rc_r.at[1, 1], core_nb)
+    for k in chunks:
+        r = row_of((e + k) % experts)
+        got(from_x.at[1, r], rx_s.at[1, k], rx_r.at[1, k], x_nb)
+        to_y[r, :] = (
+            part[1, 2 * x + c, r, :].astype(F32)
+            + from_core[1, 1, r, :].astype(F32)
+            + from_x[1, r, :].astype(F32)
+        ).astype(BF16)
+        put(to_y.at[r], from_y.at[r], ry_s.at[k], ry_r.at[k], y_nb)
+    got(from_core.at[0, 1], rc_s.at[0, 1], rc_r.at[0, 1], core_nb)
+    for k in chunks:
+        r = row_of((e + k) % experts)
+        got(from_x.at[0, r], rx_s.at[0, k], rx_r.at[0, k], x_nb)
+        got(from_y.at[r], ry_s.at[k], ry_r.at[k], y_nb)
+        value = (
+            part[0, 2 * x + c, r, :].astype(F32)
+            + from_core[0, 1, r, :].astype(F32)
+            + from_x[0, r, :].astype(F32)
+            + from_y[r, :].astype(F32)
+        ).astype(BF16)
+        if k == 0:
+            ret[e] = value
+        else:
+            final[k] = value
+            put(final.at[k], ret.at[e], rz_s.at[k], rz_r.at[k], z_nb[k])
+    for k in range(1, experts):
+        got(ret.at[came[k]], rz_s.at[k], rz_r.at[k], z_nb[k])
+    for copy in sent:
+        copy.wait_send()
+
+
+def expert_call(ob, gate_rows, up_rows, down_rows, block_rows, scale):
+    experts, rows, width = ob.shape
+    hidden_rows = gate_rows.shape[0]
+    every = experts * rows
+    cols = width // 4
+    dma = pltpu.SemaphoreType.DMA
+    vmem = pl.BlockSpec(memory_space=pltpu.VMEM)
+    hbm = pl.BlockSpec(memory_space=pl.ANY)
+    return pl.pallas_call(
+        functools.partial(expert_kernel, experts, rows, scale),
+        out_shape=(
+            jax.ShapeDtypeStruct((experts, rows, cols), BF16),
+            jax.ShapeDtypeStruct((block_rows, width), BF16),
+        ),
+        in_specs=[vmem, hbm, hbm, hbm],
+        out_specs=(vmem, vmem),
+        scratch_shapes=[
+            pltpu.VMEM((2, every, width), BF16),
+            pltpu.VMEM((hidden_rows, width), BF16),
+            pltpu.VMEM((hidden_rows, width), BF16),
+            pltpu.VMEM((hidden_rows, width), BF16),
+            pltpu.VMEM((every, hidden_rows), BF16),
+            pltpu.VMEM((2, 4, every, cols), BF16),
+            pltpu.VMEM((2, 2, every, cols), BF16),
+            pltpu.VMEM((2, every, cols), BF16),
+            pltpu.VMEM((2, every, cols), BF16),
+            pltpu.VMEM((every, cols), BF16),
+            pltpu.VMEM((every, cols), BF16),
+            pltpu.VMEM((experts, rows, cols), BF16),
+            pltpu.VMEM((2, block_rows, every), BF16),
+            dma((3,)), dma,
+            dma((experts,)), dma((experts,)), dma((experts,)), dma((experts,)),
+            dma((2, experts)), dma((2, experts)), dma((2, experts)), dma((2, experts)),
+            dma((2, experts)), dma((2, experts)),
+            dma((2, 2)), dma((2, 2)), dma((2, experts)), dma((2, experts)),
+            dma((experts,)), dma((experts,)), dma((experts,)), dma((experts,)),
+        ],
+        compiler_params=pltpu.CompilerParams(
+            collective_id=0, has_side_effects=True, vmem_limit_bytes=56 * 1024 * 1024
+        ),
+    )(ob, gate_rows, up_rows, down_rows)
+
+
+def on_device_fused(tokens, routes, router, gate_weight, up_weight, down_weight):
+    micro_count, rows_dev, model_width = tokens.shape
+    experts = router.shape[1]
+    capacity = 9 * rows_dev // (4 * experts)
+    padded = -(-capacity // 8) * 8
+    section_count = lax.axis_size("section")
+    replicas = lax.axis_size("dp")
+    col_width = model_width // section_count
+    logits = jnp.einsum("mtd,de->mte", tokens, router, preferred_element_type=F32)
+    named = routes[..., None] == jnp.arange(experts, dtype=jnp.int32)
+    chosen = jnp.sum(jnp.where(named, logits[:, :, None, :], 0.0), axis=-1)
+    logit_gap = chosen[..., 0] - chosen[..., 1]
+    first_gate = jax.nn.sigmoid(logit_gap)
+    second_gate = jax.nn.sigmoid(-logit_gap)
+    target = jax.vmap(lambda one_block: route_targets(one_block, experts, padded))(routes)
+    hot = (
+        jnp.arange(experts * padded, dtype=jnp.int32).reshape(experts, 1, 1, padded, 1)
+        == target.transpose(2, 0, 1)[None, :, :, None, :]
+    )
+    placing = (hot[:, 0] | hot[:, 1]).astype(BF16)
+    outgoing = jnp.einsum("emst,mtd->emsd", placing, tokens, preferred_element_type=F32)
+    outgoing = outgoing.astype(BF16).reshape(experts, micro_count * padded, model_width)
+    all_tokens = rows_dev * lax.axis_size("expert") * replicas
+    gram_scale = experts / (2.0 * micro_count * all_tokens)
+    returned, gram_block = expert_call(
+        outgoing, gate_weight[0], up_weight[0], down_weight[0], col_width // replicas, gram_scale
+    )
+    back = returned.reshape(experts, micro_count, padded, col_width)
+    picked = jnp.einsum(
+        "ekmst,emsd->kmtd", hot.astype(BF16), back, preferred_element_type=F32
+    )
+    own_cols = lax.dynamic_slice_in_dim(
+        tokens, lax.axis_index("section") * col_width, col_width, 2
+    ).astype(F32)
+    layer_out = (
+        own_cols + first_gate[..., None] * picked[0] + second_gate[..., None] * picked[1]
+    ).astype(BF16)
+    return (layer_out, gram_block[None])
+
+
 def solution(mesh):
+    sizes = dict(mesh.shape)
+    fused = sizes["section"] == 4 and sizes["dp"] == 2
     return jax.shard_map(
-        on_device,
+        on_device_fused if fused else on_device,
         mesh=mesh,
         in_specs=(
             P(None, ("expert", "dp"), None),

time: 225 us -> 85 us (0.38)
  waiting for transfers between devices: 106 us -> 0 us
  Pallas kernels: 0 us -> 72.6 us
  blocking collectives: 47.3 us -> 0 us
  matrix products: 31.4 us -> 3.76 us
  between operations: 13.9 us -> 0.74 us
  local copies, waits for them, and re-layouts: 13.6 us -> 5.79 us
  other arithmetic: 7.26 us -> 1.75 us
  starting transfers between devices: 4.9 us -> 0 us
    pallas_call x0 -> x1, Pallas kernels: none -> 72.6 us  [expert_call(): pl.pallas_call(functools.partial(expert_kernel, experts, rows, scale), ou...]
    reduce_scatter x2 -> x0, waiting for transfers between devices: 57.3 us -> none  [the longest x1 40.4 us: on_device(): lax.psum_scatter(partial_out.astype(jnp.bfloat16), 'section', scatter_dim...]
    all_gather x1 -> x0, waiting for transfers between devices: 48.7 us -> none  [on_device(): rows_both = lax.all_gather(rows_all, 'dp', axis=0, tiled=True)]
    all_to_all x1 -> x0, blocking collectives: 47.3 us -> none  [on_device(): lax.all_to_all(outgoing, 'expert', split_axis=1, concat_axis=1, tiled=True)]
    dot_general x5 -> x3, matrix products: 31.3 us -> 3.63 us  [the longest x1 1.79 us: on_device_fused(): jnp.einsum('emst,mtd->emsd', placing, tokens, preferred_element_type=F32)]
    gather x9 -> x0, local copies, waits for them, and re-layouts: 6.39 us -> none  [the longest x5 3.25 us: on_device(): chosen = jnp.take_along_axis(logits, routes, axis=-1)]
    reduce_sum x2 -> x1, other arithmetic: 5.56 us -> 0.04 us  [on_device_fused(): chosen = jnp.sum(jnp.where(named, logits[:, :, None, :], 0.0), axis=-1)]
    all_to_all x1 -> x0, starting transfers between devices: 4.6 us -> none  [on_device(): lax.all_to_all(expert_out, 'expert', split_axis=1, concat_axis=1, tiled=T...]
  transfers between devices with their start and end apart: 4 -> 0, of which waited for: 4 -> 0; matrix products, arithmetic and copies ran while one was open for 7% -> 0% of each run, Pallas kernels for 0% -> 0%
where the time goes in v2:
time: 85 us; the launch traced here: 84.7 us
  Pallas kernels  72.6 us (85%)
  local copies, waits for them, and re-layouts  5.79 us (7%)
  matrix products  3.76 us (4%)
  other arithmetic  1.75 us (2%)
    pallas_call x1, Pallas kernels, expert_call(): pl.pallas_call(functools.partial(expert_kernel, experts, rows, scale), ou...  72.6 us
    unnamed x8, local copies, waits for them, and re-layouts  4.02 us
    dot_general x1, matrix products, on_device_fused(): jnp.einsum('emst,mtd->emsd', placing, tokens, preferred_element_type=F32)  1.79 us

profile of v2, /device:TPU:0, one launch (start us, length us, event | category | flops | bytes accessed | tf_op | source)
XLA Modules:
  0.0 84.7 jit_solution(3917357206166483384)
XLA Ops:
  0.6 0.0 copy-start
  0.6 0.8 copy.29
  1.4 0.1 eq.46
  1.6 0.1 fusion.11
  1.8 0.1 reshape.45
  1.9 0.1 copy.30
  2.0 0.7 add_bitcast_fusion
  2.7 0.1 broadcast_compare_fusion
  2.8 1.8 %fusion = bf16[4,2,40,3072]{3,2,0,1:T(8,128)(2,1)S(1)} fusion(bf16[2,64,3072]{2,1,0:T(8,128)(2,1)} %param.6, pred[4,2,2,40,64]{4,3,0,1,2:T(8,128)(4,1)S(1)} %broadcast_compare_fusion), kind=kOutput, calls=%fused_computation.1 | convolution fusion | flops 126832640 | bytes 2793472 | tf_op jit(solution)/shard_map/emst,mtd->emsd/dot_general | solution.py:362
  4.6 1.4 %copy.31 = bf16[4,2,40,3072]{3,2,1,0:T(8,128)(2,1)} copy(bf16[4,2,40,3072]{3,2,0,1:T(8,128)(2,1)S(1)} %fusion) | data formatting | bytes 3932160 | tf_op jit(solution)/shard_map/convert_element_type | solution.py:363
  6.0 0.0 copy-start.1
  6.0 0.0 copy-start.2
  6.0 72.6 %shard_map.77 = (bf16[4,80,768]{2,1,0:T(8,128)(2,1)}, bf16[384,3072]{1,0:T(8,128)(2,1)}) custom-call(bf16[4,80,3072]{2,1,0:T(8,128)(2,1)} %bitcast.58, bf16[1024,3072]{1,0:T(8,128)(2,1)} %bitcast.59, bf16[1024,3072]{1,0:T(8,128)(2,1)} %bitcast.60, bf16[1024,3072]{1,0:T(8,128)(2,1)} %bitcast.61), custom_call_target="tpu_custom_call" | custom-call | tf_op jit(solution)/shard_map/pallas_call | solution.py:307
  78.6 1.4 %convolution_bitcast_fusion = f32[2,2,64,768]{3,2,0,1:T(8,128)S(1)} fusion(bf16[4,2,40,768,1]{3,2,1,0,4:T(8,128)(2,1)} %bitcast.63, s32[2,2,64]{2,0,1:T(2,128)S(1)} %add_bitcast_fusion, s32[4,40]{1,0:T(4,128)S(1)} %multiply_add_fusion), kind=kOutput, calls=%fused_computation.2 | convolution fusion | flops 62955520 | bytes 1279616 | tf_op jit(solution)/shard_map/ekmst,emsd->kmtd/dot_general | solution.py:370
  80.1 0.0 copy-done
  80.1 0.0 copy-done.1
  80.1 0.4 fusion.12
  80.5 0.0 copy-done.2
  80.6 0.8 %fusion.5 = bf16[2,64,768]{2,1,0:T(8,128)(2,1)} fusion(f32[2,2,64,768]{3,2,0,1:T(8,128)S(1)} %convolution_bitcast_fusion, f32[2,64]{1,0:T(2,128)S(1)} %bitcast.65, f32[2,64]{1,0:T(2,128)S(1)} %bitcast.66, bf16[2,64,3072]{2,1,0:T(8,128)(2,1)S(1)} %copy-done.1, s32[]{:T(128)S(6)} %select_n.7), kind=kLoop, calls=%fused_computation.8 | loop fusion | flops 589824 | bytes 1180676 | tf_op jit(solution)/shard_map/convert_element_type | solution.py:378
  81.4 3.2 %copy.43 = bf16[1,384,3072]{2,1,0:T(8,128)(2,1)} copy(bf16[1,384,3072]{2,1,0:T(8,128)(2,1)} %bitcast.62) | data formatting | bytes 4718592
  (6 shorter events, 0.1 us)
Async XLA Ops:
  0.6 79.5 %copy-start = (bf16[3072,4]{0,1:T(4,128)(2,1)S(1)}, bf16[3072,4]{0,1:T(4,128)(2,1)}, u32[]{:S(2)}) copy-start(bf16[3072,4]{0,1:T(4,128)(2,1)} %param.8) | copy-start | bytes 73732
  6.0 74.1 %copy-start.1 = (bf16[2,64,3072]{2,1,0:T(8,128)(2,1)S(1)}, bf16[2,64,3072]{2,1,0:T(8,128)(2,1)}, u32[]{:S(2)}) copy-start(bf16[2,64,3072]{2,1,0:T(8,128)(2,1)} %param.6) | copy-start | bytes 2359300
  6.0 74.5 %copy-start.2 = (s32[2,64,2]{1,2,0:T(2,128)S(1)}, s32[2,64,2]{1,2,0:T(2,128)}, u32[]{:S(2)}) copy-start(s32[2,64,2]{1,2,0:T(2,128)} %param.7) | copy-start | bytes 3076

commit v3 on v2

--- a/solution.py
+++ b/solution.py
@@ -98,9 +98,9 @@
 
 
 def expert_kernel(
-    experts, rows, scale, ob, gate_hbm, up_hbm, down_hbm, ret, gram,
-    xin, gate_v, up_v, down_v, inner, part, from_core, to_x, from_x, to_y, from_y, final, left_t,
-    w_sem, l_sem, z_s, z_r, y_s, y_r, x_s, x_r, c_s, c_r, d_s, d_r, rc_s, rc_r, rx_s, rx_r, ry_s, ry_r, rz_s, rz_r,
+    experts, rows, scale, ob, gate_hbm, up_hbm, down_hbm, ret, gram_hbm,
+    xin, gate_v, up_v, down_v, inner, part, from_core, to_x, from_x, to_y, from_y, final, left_t, gram,
+    w_sem, l_sem, g_sem, z_s, z_r, y_s, y_r, x_s, x_r, c_s, c_r, d_s, d_r, rc_s, rc_r, rx_s, rx_r, ry_s, ry_r, rz_s, rz_r,
 ):
     width = ob.shape[2]
     half, third = width // 2, width // 6
@@ -263,6 +263,8 @@
         return carry
 
     lax.fori_loop(0, width // tile, gram_step, 0)
+    gram_copy = pltpu.make_async_copy(gram, gram_hbm, g_sem)
+    gram_copy.start()
 
     got(from_core.at[1, 1], rc_s.at[1, 1], rc_r.at[1, 1], core_nb)
     for k in chunks:
@@ -294,6 +296,7 @@
         got(ret.at[came[k]], rz_s.at[k], rz_r.at[k], z_nb[k])
     for copy in sent:
         copy.wait_send()
+    gram_copy.wait()
 
 
 def expert_call(ob, gate_rows, up_rows, down_rows, block_rows, scale):
@@ -311,7 +314,7 @@
             jax.ShapeDtypeStruct((block_rows, width), BF16),
         ),
         in_specs=[vmem, hbm, hbm, hbm],
-        out_specs=(vmem, vmem),
+        out_specs=(vmem, hbm),
         scratch_shapes=[
             pltpu.VMEM((2, every, width), BF16),
             pltpu.VMEM((hidden_rows, width), BF16),
@@ -326,7 +329,8 @@
             pltpu.VMEM((every, cols), BF16),
             pltpu.VMEM((experts, rows, cols), BF16),
             pltpu.VMEM((2, block_rows, every), BF16),
-            dma((3,)), dma,
+            pltpu.VMEM((block_rows, width), BF16),
+            dma((3,)), dma, dma,
             dma((experts,)), dma((experts,)), dma((experts,)), dma((experts,)),
             dma((2, experts)), dma((2, experts)), dma((2, experts)), dma((2, experts)),
             dma((2, experts)), dma((2, experts)),
@@ -354,22 +358,25 @@
     first_gate = jax.nn.sigmoid(logit_gap)
     second_gate = jax.nn.sigmoid(-logit_gap)
     target = jax.vmap(lambda one_block: route_targets(one_block, experts, padded))(routes)
-    hot = (
-        jnp.arange(experts * padded, dtype=jnp.int32).reshape(experts, 1, 1, padded, 1)
-        == target.transpose(2, 0, 1)[None, :, :, None, :]
-    )
-    placing = (hot[:, 0] | hot[:, 1]).astype(BF16)
-    outgoing = jnp.einsum("emst,mtd->emsd", placing, tokens, preferred_element_type=F32)
-    outgoing = outgoing.astype(BF16).reshape(experts, micro_count * padded, model_width)
+    micro = jnp.arange(micro_count, dtype=jnp.int32)[:, None, None]
+    chosen_slot = target % padded
+    wanted = ((routes * micro_count + micro) * padded + chosen_slot).reshape(-1, 2)
+    places = jnp.arange(experts * micro_count * padded, dtype=jnp.int32)
+    placing = (
+        (places[:, None] == wanted[None, :, 0]) | (places[:, None] == wanted[None, :, 1])
+    ).astype(BF16)
+    outgoing = jnp.dot(
+        placing, tokens.reshape(-1, model_width), preferred_element_type=F32
+    ).astype(BF16).reshape(experts, micro_count * padded, model_width)
     all_tokens = rows_dev * lax.axis_size("expert") * replicas
     gram_scale = experts / (2.0 * micro_count * all_tokens)
     returned, gram_block = expert_call(
         outgoing, gate_weight[0], up_weight[0], down_weight[0], col_width // replicas, gram_scale
     )
-    back = returned.reshape(experts, micro_count, padded, col_width)
-    picked = jnp.einsum(
-        "ekmst,emsd->kmtd", hot.astype(BF16), back, preferred_element_type=F32
-    )
+    back = returned.reshape(-1, col_width)
+    taking = (wanted.T[:, :, None] == places).astype(BF16).reshape(-1, places.shape[0])
+    picked = jnp.dot(taking, back, preferred_element_type=F32)
+    picked = picked.reshape(2, micro_count, rows_dev, col_width)
     own_cols = lax.dynamic_slice_in_dim(
         tokens, lax.axis_index("section") * col_width, col_width, 2
     ).astype(F32)

time: 85 us -> 84.4 us (level)
  local copies, waits for them, and re-layouts: 5.79 us -> 3.6 us
  matrix products: 3.76 us -> 5.19 us
  other arithmetic: 1.75 us -> 2.74 us
    unnamed x8 -> x10, local copies, waits for them, and re-layouts: 4.02 us -> 2.21 us
    dot_general x2, matrix products: 3.23 us -> 4.65 us  [the longest x1 3.07 us: on_device_fused(): jnp.dot(placing, tokens.reshape(-1, model_width), preferred_element_type=...]
    convert_element_type x1 -> x0, local copies, waits for them, and re-layouts: 1.4 us -> none  [on_device_fused(): outgoing.astype(BF16).reshape(experts, micro_count * padded, model_width)]
    convert_element_type x1, other arithmetic: 0.85 us -> 1.94 us  [on_device_fused(): layer_out = (own_cols + first_gate[..., None] * picked[0] + second_gate[....]
    slice x0 -> x1, local copies, waits for them, and re-layouts: none -> 0.93 us  [on_device_fused(): picked[0]]
where the time goes in v3:
time: 84.4 us; the launch traced here: 84.1 us
  Pallas kernels  71.8 us (85%)
  matrix products  5.19 us (6%)
  local copies, waits for them, and re-layouts  3.6 us (4%)
  other arithmetic  2.74 us (3%)
    pallas_call x1, Pallas kernels, expert_call(): pl.pallas_call(functools.partial(expert_kernel, experts, rows, scale), ou...  71.8 us
    dot_general x1, matrix products, on_device_fused(): jnp.dot(placing, tokens.reshape(-1, model_width), preferred_element_type=...  3.07 us
    unnamed x10, local copies, waits for them, and re-layouts  2.21 us
    convert_element_type x1, other arithmetic, on_device_fused(): layer_out = (own_cols + first_gate[..., None] * picked[0] + second_gate[....  1.94 us

profile of v3, /device:TPU:0, one launch (start us, length us, event | category | flops | bytes accessed | tf_op | source)
XLA Modules:
  0.0 84.1 jit_solution(8456916488355903270)
XLA Ops:
  0.6 0.0 copy-start
  0.6 0.8 copy.26
  1.4 0.1 eq.80
  1.6 0.1 fusion.6
  1.8 0.1 reshape.34
  1.9 0.1 copy.27
  2.0 0.7 fusion.10
  2.7 0.1 reshape.35
  2.8 3.1 %convolution_convert_fusion = bf16[320,3072]{1,0:T(8,128)(2,1)} fusion(bf16[128,3072]{1,0:T(8,128)(2,1)} %bitcast.39, s32[128]{0:T(128)S(1)} %get-tuple-element.11, s32[128]{0:T(128)S(1)} %get-tuple-element.10), kind=kOutput, calls=%fused_computation | convolution fusion | flops 252764160 | bytes 2753536 | tf_op jit(solution)/shard_map/dot_general | solution.py:368
  5.9 0.0 copy-start.1
  5.9 0.0 copy-start.3
  5.9 71.8 %shard_map.77 = (bf16[4,80,768]{2,1,0:T(8,128)(2,1)}, bf16[384,3072]{1,0:T(8,128)(2,1)}) custom-call(bf16[4,80,3072]{2,1,0:T(8,128)(2,1)} %bitcast.35, bf16[1024,3072]{1,0:T(8,128)(2,1)} %bitcast.36, bf16[1024,3072]{1,0:T(8,128)(2,1)} %bitcast.37, bf16[1024,3072]{1,0:T(8,128)(2,1)} %bitcast.38), custom_call_target="tpu_custom_call" | custom-call | tf_op jit(solution)/shard_map/pallas_call | solution.py:310
  77.7 0.0 copy-start.2
  77.7 1.6 %fusion = f32[256,768]{1,0:T(8,128)S(1)} fusion(bf16[320,768]{1,0:T(8,128)(2,1)} %bitcast.43, s32[256]{0:T(256)S(1)} %bitcast.44), kind=kOutput, calls=%fused_computation.3 | convolution fusion | flops 125911040 | bytes 1278976 | tf_op jit(solution)/shard_map/dot_general | solution.py:378
  79.3 0.9 %fusion.11 = (f32[128,768]{1,0:T(8,128)}, f32[128,768]{1,0:T(8,128)}) fusion(f32[256,768]{1,0:T(8,128)S(1)} %fusion), kind=kLoop, calls=%fused_computation.27 | loop fusion | bytes 1572864 | tf_op jit(solution)/shard_map/slice | solution.py:384
  80.3 0.0 copy-done
  80.3 0.0 copy-done.1
  80.3 0.4 fusion.7
  80.7 0.0 copy-done.3
  80.7 1.9 %add_convert_fusion = bf16[2,64,768]{2,1,0:T(8,128)(2,1)} fusion(f32[2,64,768]{2,1,0:T(8,128)} %bitcast.42, f32[2,64,768]{2,1,0:T(8,128)} %bitcast.41, f32[2,64]{1,0:T(2,128)S(1)} %bitcast.46, f32[2,64]{1,0:T(2,128)S(1)} %bitcast.47, bf16[2,64,3072]{2,1,0:T(8,128)(2,1)S(1)} %copy-done.1, s32[]{:T(128)S(6)} %select_n.14), kind=kLoop, calls=%fused_computation.1 | loop fusion | flops 589824 | bytes 1180676 | tf_op jit(solution)/shard_map/convert_element_type | solution.py:385
  82.7 0.0 copy-done.2
  82.7 1.4 %copy.30 = bf16[1,384,3072]{2,1,0:T(8,128)(2,1)} copy(bf16[1,384,3072]{2,1,0:T(8,128)(2,1)S(1)} %bitcast.40) | data formatting | bytes 4718592
  (7 shorter events, 0.1 us)
Async XLA Ops:
  0.6 79.6 %copy-start = (bf16[3072,4]{0,1:T(4,128)(2,1)S(1)}, bf16[3072,4]{0,1:T(4,128)(2,1)}, u32[]{:S(2)}) copy-start(bf16[3072,4]{0,1:T(4,128)(2,1)} %param.8) | copy-start | bytes 73732
  5.9 74.4 %copy-start.1 = (bf16[2,64,3072]{2,1,0:T(8,128)(2,1)S(1)}, bf16[2,64,3072]{2,1,0:T(8,128)(2,1)}, u32[]{:S(2)}) copy-start(bf16[2,64,3072]{2,1,0:T(8,128)(2,1)} %param.6) | copy-start | bytes 2359300
  5.9 74.8 %copy-start.3 = (s32[2,64,2]{1,2,0:T(2,128)S(1)}, s32[2,64,2]{1,2,0:T(2,128)}, u32[]{:S(2)}) copy-start(s32[2,64,2]{1,2,0:T(2,128)} %param.7) | copy-start | bytes 3076
  77.7 5.0 %copy-start.2 = (bf16[384,3072]{1,0:T(8,128)(2,1)S(1)}, bf16[384,3072]{1,0:T(8,128)(2,1)}, u32[]{:S(2)}) copy-start(bf16[384,3072]{1,0:T(8,128)(2,1)} %get-tuple-element.5) | copy-start | bytes 7077892
